TPU v7x, 256 devices: a whole 4x4x8 slice. The times are simulated.
256 devices in a mesh: lon: 32 (over z, y), lat: 8 (over x, core).
Axes of the slice: x: 4, y: 4, z: 8, core: 2. Of those that a mesh axis runs over, the one named last changes fastest.
Arguments:
- right_side: float32 [2048, 16384], P('lat', 'lon'), may hold values from -6 to 6
- depth_level: int32 [2048, 16384], P('lat', 'lon'), may hold values from 1 to 50
- ocean_mask: int32 [2048, 16384], P('lat', 'lon'), may hold values 0 or 1
Outputs:
- pressure: float32 [2048, 16384], P('lat', 'lon')
- residual: float32 [2048, 16384], P('lat', 'lon')
All inputs are finite; a program needn't handle non-finite values. No bound on the sum of `ocean_mask` on one device may be relied on, other than what follows from the above.
Results may differ from a plain program's by a relative error of at most 0.0003.
Values sent between devices are 32-bit elements; how exact they have to be, the bound alone decides.
No kernel may reach another device: no remote copies, remote signals or barrier semaphores. Data moves between devices by JAX's collectives and lax.ppermute only.
A program may use at most 128 MiB of HBM per device.

v0:
```python
import jax
import jax.numpy as jnp
import numpy as np
from jax import lax
from jax.experimental import pallas as pl
from jax.experimental.pallas import tpu as pltpu
from jax.sharding import PartitionSpec as P

LEVELS = 4
COARSE_SWEEPS = 9
DEPTH_LEVELS = 50
OMEGA = 0.8
SIGMA = 1e-05

CELL = 2 ** (LEVELS - 1)
LANES = 128
SIDE = 96
LEAD = 16
ROWS = 32
COLS = 64
TALL = ROWS + 8


def east(x):
    return pltpu.roll(x, x.shape[1] - 1, 1)


def west(x):
    return pltpu.roll(x, 1, 1)


def north(x):
    return pltpu.roll(x, x.shape[0] - 1, 0)


def south(x):
    return pltpu.roll(x, 1, 0)


def row_of(x):
    return lax.broadcasted_iota(jnp.int32, x.shape, 0)


def lane_of(x):
    return lax.broadcasted_iota(jnp.int32, x.shape, 1)


class Whole:
    def __init__(self, inner, strip, count=TALL):
        self.inner, self.strip, self.count = inner, strip, count

    def __getitem__(self, at):
        q, r = at
        parts = [self.strip[q, r, 16:24, :], self.inner[q, r, 8:24, :], self.strip[q, r, 0 : self.count - 24, :]]
        return jnp.concatenate(parts, axis=0)


def strip_of(x):
    return jnp.concatenate([x[24:TALL], x[0:8]], axis=0)


def merged(inner, strip):
    low = jnp.where(row_of(strip[0:8]) < 2, strip[16:24], inner[0:8])
    high = jnp.where(row_of(strip[0:8]) >= 6, strip[0:8], inner[24:32])
    return jnp.concatenate([low, inner[8:24], high, strip[8:16]], axis=0)


def close(v, n):
    for r in range(n):
        v[0, r] = south(v[n, r])
        v[n + 1, r] = north(v[1, r])


def find_faces(n, h, ke, kn):
    for q in range(n):
        for r in range(n):
            here = h[q, r]
            ke[q, r] = jnp.minimum(here, h[q, r + 1] if r + 1 < n else east(h[q, 0]))
            kn[q + 1, r] = jnp.minimum(here, h[q + 1, r])


def weigh(faces, source):
    diagonal = SIGMA + faces
    return diagonal, OMEGA / diagonal, jnp.where(faces > 0.0, source, 0.0)


def find_weights(n, ke, kn, source, d, w, s, v):
    for q in range(n):
        for r in range(n):
            kw = ke[q, r - 1] if r else west(ke[q, n - 1])
            faces = (ke[q, r] + kw) + (kn[q + 1, r] + kn[q, r])
            diagonal, weight, kept = weigh(faces, source[q, r])
            d[q, r], w[q, r], s[q, r] = diagonal, weight, kept
            v[q + 1, r] = weight * kept
    close(v, n)


def pull(n, ke, kn, v, q, count=None):
    ks = [ke[q, r] for r in range(n)]
    cs = [v[q + 1, r][:count] for r in range(n)]
    out = []
    for r in range(n):
        kw = ks[r - 1] if r else west(ks[n - 1])
        ve = cs[r + 1] if r + 1 < n else east(cs[0])
        vw = cs[r - 1] if r else west(cs[n - 1])
        out.append((ks[r] * ve + kw * vw) + (kn[q + 1, r] * v[q + 2, r][:count] + kn[q, r] * v[q, r][:count]))
    return cs, out


def sweep(n, ke, kn, w, s, v, out, also=None):
    for q in range(n):
        cs, total = pull(n, ke, kn, v, q)
        for r in range(n):
            new = (1.0 - OMEGA) * cs[r] + w[q, r] * (s[q, r] + total[r])
            out[q + 1, r] = new
        if also is not None:
            also(q, [out[q + 1, r][:ROWS] for r in range(n)])
    close(out, n)


def remains(n, ke, kn, d, s, v, q, count=None):
    cs, total = pull(n, ke, kn, v, q, count)
    return [(s[q, r] - d[q, r] * cs[r]) + total[r] for r in range(n)]


def restrict(n, ke, kn, d, s, v, put):
    for q in range(n // 2):
        a = remains(n, ke, kn, d, s, v, 2 * q)
        b = remains(n, ke, kn, d, s, v, 2 * q + 1)
        for r in range(n // 2):
            put(q, r, 0.25 * ((a[2 * r] + a[2 * r + 1]) + (b[2 * r] + b[2 * r + 1])))


def coarsen(n, h, put):
    for q in range(n // 2):
        for r in range(n // 2):
            a = h[2 * q, 2 * r] + h[2 * q, 2 * r + 1]
            b = h[2 * q + 1, 2 * r] + h[2 * q + 1, 2 * r + 1]
            put(q, r, 0.0625 * (a + b))


def dot_parts(x, matrix, parts):
    out = 0.0
    for part in range(parts):
        piece = x.astype(jnp.bfloat16)
        out = out + jnp.dot(piece, matrix, preferred_element_type=jnp.float32)
        if part + 1 < parts:
            x = x - piece.astype(jnp.float32)
    return out


def fold(blocks, free):
    return [jnp.where(free, pltpu.roll(blocks[3], 96 - 32 * i, 1), blocks[i]) for i in range(3)]


def unfold(three, first):
    lane = lane_of(three[0])
    a, b, c = (pltpu.roll(x, 32 * (i + 1), 1) for i, x in enumerate(three))
    return list(three) + [jnp.where(lane < first + 32, a, jnp.where(lane < first + 64, b, c))]


def by_parity(axis, fill, first, second):
    even = lax.rem(lax.axis_index(axis), 2) == 0

    @pl.when(even)
    def _():
        fill(first, second)

    @pl.when(jnp.logical_not(even))
    def _():
        fill(second, first)


def pack_kernel(f, depth, mask, first, second, fs, ds, ms, sems):
    last = f.shape[1] - LANES
    copies = []
    for j, column in enumerate((0, last)):
        for i, (source, to) in enumerate(((f, fs), (depth, ds), (mask, ms))):
            copies.append(pltpu.make_async_copy(source.at[:, column : column + LANES], to.at[j], sems.at[j, i]))
    for copy in copies:
        copy.start()
    for copy in copies:
        copy.wait()

    def fill(to_next, to_previous):
        for j, to in enumerate((to_previous, to_next)):
            count = ROWS * CELL // 4
            s_blocks, h_blocks = [], []
            for block in range(4):
                s_rows, h_rows = [], []
                for q in (2 * block, 2 * block + 1):
                    rows = pl.ds(q, ROWS, stride=CELL)
                    s_rows.append(fs[j, rows, :])
                    h_rows.append((ds[j, rows, :] * ms[j, rows, :]).astype(jnp.float32))
                s_blocks.append(jnp.concatenate(s_rows, axis=0))
                h_blocks.append(jnp.concatenate(h_rows, axis=0))
            lane = lane_of(s_blocks[0])
            free = lane < LANES - SIDE if j else lane >= SIDE
            for k, blocks in enumerate((s_blocks, h_blocks)):
                for i, x in enumerate(fold(blocks, free)):
                    to[k, i * count : (i + 1) * count, :] = x

    by_parity("lon", fill, first, second)


def own_kernel(f, depth, mask, split, s0, h0, nat_s, nat_h):
    matrix = split[...]
    tiles = nat_s.shape[0]
    for c in range(tiles):
        lanes = slice(c * LANES, (c + 1) * LANES)
        nat_s[c] = f[:, lanes]
        nat_h[c] = (depth[:, lanes] * mask[:, lanes]).astype(jnp.float32)
    for nat, out, parts in ((nat_s, s0, 3), (nat_h, h0, 1)):
        rows = [
            jnp.concatenate([nat[c, pl.ds(q, ROWS, stride=CELL), :] for c in range(tiles)], axis=1) for q in range(CELL)
        ]
        x = dot_parts(jnp.concatenate(rows, axis=0), matrix, parts)
        for q in range(CELL):
            for r in range(CELL):
                out[q, r] = x[q * ROWS : (q + 1) * ROWS, r * LANES : (r + 1) * LANES]


def down_kernel(
    first, second, s_own, h_own, split,
    s0, h0, s1, h1, s2, h2, s3, it0, it1, it2,
    ke0, kn0, d0, w0, k0, ke1, kn1, d1, w1, k1, ke2, kn2, d2, w2, k2, out_first, out_second,
    v0, v1, v2,
):
    even = lax.rem(lax.axis_index("lon"), 2) == 0
    matrix = split[...]
    count = ROWS * CELL // 4

    def sides(k):
        before, after = [], []
        for i in range(3):
            rows = slice(i * count, (i + 1) * count)
            a, b = first[k, rows, :], second[k, rows, :]
            before.append(jnp.where(even, b, a))
            after.append(jnp.where(even, a, b))
        before = jnp.concatenate(unfold(before, LANES - SIDE), axis=0)
        after = jnp.concatenate(unfold(after, 0), axis=0)
        return jnp.concatenate([before, after], axis=1)

    for k, own, out, parts in ((0, s_own, s0, 3), (1, h_own, h0, 1)):
        x = dot_parts(sides(k), matrix, parts)
        for q in range(CELL):
            for r in range(CELL):
                y = own[q, r] + x[q * ROWS : (q + 1) * ROWS, r * LANES : (r + 1) * LANES]
                out[q, r] = y * (1.0 / DEPTH_LEVELS) if k else y

    def put(ref):
        def at(q, r, x):
            ref[q, r] = x

        return at

    last = []
    levels = (
        (8, h0, ke0, kn0, s0, d0, w0, k0, v0, it0, put(s1), put(h1)),
        (4, h1, ke1, kn1, s1, d1, w1, k1, v1, it1, put(s2), put(h2)),
        (2, h2, ke2, kn2, s2, d2, w2, k2, v2, it2, lambda q, r, x: last.append(x), lambda q, r, x: last.append(x)),
    )
    for n, h, ke, kn, source, d, w, k, v, it, put_s, put_h in levels:
        for r in range(n):
            h[n, r] = north(h[0, r])
        find_faces(n, h, ke, kn)
        for r in range(n):
            kn[0, r] = south(kn[n, r])
        find_weights(n, ke, kn, source, d, w, k, v)
        sweep(n, ke, kn, w, k, v, it)
        restrict(n, ke, kn, d, k, it, put_s)
        coarsen(n, h, put_h)
    s, h = last
    s3[0], s3[1] = s, h

    def send(to, low, blocks):
        rows = slice(0, 8) if low else slice(ROWS - 8, ROWS)
        for q in range(CELL):
            for g in range(2):
                four = []
                for r in range(4 * g, 4 * g + 4):
                    a, b = s0[q, r, rows, :], pltpu.roll(h0[q, r, rows, :], 4, 0)
                    four.append(jnp.where(row_of(a) < 4, a, b) if low else jnp.where(row_of(a) < 4, b, a))
                for i, x in enumerate(fold(four, lane_of(four[0]) >= SIDE)):
                    to[6 * q + 3 * g + i] = x
        for i, x in enumerate(blocks):
            to[6 * CELL + i] = x

    def fill(to_next, to_previous):
        send(to_next, False, (s[24:32], s[16:24], h[24:32], h[16:24]))
        send(to_previous, True, (s[0:8], s[8:16], h[0:8], h[8:16]))

    by_parity("lat", fill, out_first, out_second)


def up_kernel(
    s0_in, h0_in, s1_in, h1_in, s2_in, h2_in, s3_in, it0_in, it1_in, it2_in,
    ke0_in, kn0_in, d0_in, w0_in, k0_in, ke1_in, kn1_in, d1_in, w1_in, k1_in, ke2_in, kn2_in, d2_in, w2_in, k2_in,
    first, second, join,
    pressure, residual,
    far, s0, h0, ke0, kn0, d0, w0, k0, e0, g0, a0, b0,
    s1, h1, ke1, kn1, d1, w1, k1, e1, g1, a1, b1, s2, h2, ke2, kn2, d2, w2, k2, e2, g2, a2, b2, flat, nat, sems,
):
    def fill(high, low):
        for q in range(CELL):
            for g in range(2):
                lows = unfold([low[6 * q + 3 * g + i] for i in range(3)], 0)
                highs = unfold([high[6 * q + 3 * g + i] for i in range(3)], 0)
                for r, a, b in zip(range(4 * g, 4 * g + 4), highs, lows):
                    s_new = jnp.where(row_of(a) < 4, a, b)
                    h_new = pltpu.roll(jnp.where(row_of(a) < 4, b, a), 4, 0)
                    for to, inner, new in ((s0, s0_in, s_new), (h0, h0_in, h_new)):
                        to[q, r, 0:8, :] = inner[q, r, ROWS - 8 : ROWS, :]
                        to[q, r, 8:16, :] = new
                        to[q, r, 16:24, :] = inner[q, r, 0:8, :]
        for i in range(4):
            far[0, i] = high[6 * CELL + i]
            far[1, i] = low[6 * CELL + i]

    by_parity("lat", fill, first, second)

    levels = (
        (8, h0, ke0, kn0, s0, d0, w0, k0, e0, g0, a0, b0, (ke0_in, kn0_in, d0_in, w0_in, k0_in), it0_in),
        (4, h1, ke1, kn1, s1, d1, w1, k1, e1, g1, a1, b1, (ke1_in, kn1_in, d1_in, w1_in, k1_in), it1_in),
        (2, h2, ke2, kn2, s2, d2, w2, k2, e2, g2, a2, b2, (ke2_in, kn2_in, d2_in, w2_in, k2_in), it2_in),
    )
    source3 = []
    for i, (n, h, ke, kn, source, d, w, k, e, g, _, _, inner, _) in enumerate(levels):
        for r in range(n):
            h[n, r] = strip_of(north(Whole((h0_in, h1_in, h2_in)[i], h)[0, r]))
        find_faces(n, h, ke, kn)
        for r in range(n):
            kn[0, r] = strip_of(south(Whole(inner[1], kn)[n, r]))
        find_weights(n, ke, kn, source, d, w, k, e)
        sweep(n, ke, kn, w, k, e, g)
        if i < 2:
            s_next, s_inner, h_next = ((s1, s1_in, h1), (s2, s2_in, h2))[i]

            def put_s(q, r, x, s_next=s_next, s_inner=s_inner):
                s_next[q, r] = strip_of(merged(s_inner[q, r], x))

            def put_h(q, r, x, h_next=h_next):
                h_next[q, r] = x

            restrict(n, ke, kn, d, k, g, put_s)
            coarsen(n, h, put_h)
        else:
            restrict(n, ke, kn, d, k, g, lambda q, r, x: source3.append(x))

    strip = source3[0]
    s = merged(s3_in[0], strip)
    row = row_of(far[0, 0])
    s = jnp.concatenate(
        [
            s[0:ROWS],
            jnp.where(row < 2, strip[8:16], far[0, 0]),
            jnp.where(row < 4, far[0, 1], far[1, 1]),
            jnp.where(row >= 6, strip[8:16], far[1, 0]),
        ],
        axis=0,
    )
    h = jnp.concatenate([s3_in[1], far[0, 2], jnp.where(row < 4, far[0, 3], far[1, 3]), far[1, 2]], axis=0)
    ke, kn = jnp.minimum(h, east(h)), jnp.minimum(h, north(h))
    kw, ks = west(ke), south(kn)
    _, weight, s = weigh((ke + kw) + (kn + ks), s)
    v = weight * s
    for _ in range(COARSE_SWEEPS - 1):
        total = (ke * east(v) + kw * west(v)) + (kn * north(v) + ks * south(v))
        v = (1.0 - OMEGA) * v + weight * (s + total)
    coarse = jnp.concatenate([v[0:ROWS], jnp.where(row < 4, v[32:40], v[48:56])], axis=0)

    above = lambda q, r: coarse
    for n, _, ke, kn, _, d, w, k, _, g, a, b, inner, it in reversed(levels):
        for q in range(n):
            for r in range(n):
                a[q + 1, r] = merged(it[q + 1, r], g[q + 1, r]) + above(q // 2, r // 2)
        close(a, n)
        ke, kn, w, k = (Whole(x, y) for x, y in zip((inner[0], inner[1], inner[3], inner[4]), (ke, kn, w, k)))
        sweep(n, ke, kn, w, k, a, b)
        if n < CELL:
            sweep(n, ke, kn, w, k, b, a)
        above = lambda q, r, a=a: a[q + 1, r]

    def flatten(q, xs):
        lane = lane_of(xs[0])
        held = (lane >= LEAD) & (lane < LEAD + COLS)
        for r in range(4):
            x = jnp.where(held, xs[r], pltpu.roll(xs[r + 4], COLS, 1))
            flat[q * ROWS : (q + 1) * ROWS, r * LANES : (r + 1) * LANES] = x

    def finish(i, out):
        copies = []
        width = 2 * LANES
        for half in range(out.shape[1] // width):
            res = dot_parts(flat[...], join[:, half * width : (half + 1) * width], 2)
            for c in (2 * half, 2 * half + 1):
                at = slice((c - 2 * half) * LANES, (c - 2 * half + 1) * LANES)
                for q in range(CELL):
                    nat[i, c, pl.ds(q, ROWS, stride=CELL), :] = res[q * ROWS : (q + 1) * ROWS, at]
                copy = pltpu.make_async_copy(nat.at[i, c], out.at[:, c * LANES : (c + 1) * LANES], sems.at[i, c])
                copy.start()
                copies.append(copy)
        return copies

    sweep(8, ke, kn, w, k, b0, a0, flatten)
    copies = finish(0, pressure)
    inner = levels[0][12]
    ke, kn, d, k = (
        Whole(x, y, ROWS) for x, y in zip((inner[0], inner[1], inner[2], inner[4]), (ke0, kn0, d0, k0))
    )
    for q in range(CELL):
        flatten(q, remains(8, ke, kn, d, k, a0, q, ROWS))
    copies += finish(1, residual)
    for copy in copies:
        copy.wait()


def swap(x, axis, count, offset, closed):
    pairs = []
    for i in range(offset, count, 2):
        if i + 1 < count or closed:
            j = (i + 1) % count
            pairs += [(i, j), (j, i)]
    return lax.ppermute(x, axis, pairs)


def own_matrix(columns):
    out = np.zeros((columns, CELL * LANES), np.float32)
    c = np.arange(columns)
    out[c, (c % CELL) * LANES + LEAD + c // CELL] = 1.0
    return jnp.asarray(out, jnp.bfloat16)


def side_matrix(columns):
    out = np.zeros((2 * LANES, CELL * LANES), np.float32)
    c = np.arange(LANES - SIDE, LANES)
    out[c, (c % CELL) * LANES + LEAD + (c - LANES) // CELL] = 1.0
    c = np.arange(SIDE)
    out[LANES + c, (c % CELL) * LANES + LEAD + (columns + c) // CELL] = 1.0
    return jnp.asarray(out, jnp.bfloat16)


def join_matrix(columns):
    out = np.zeros((4 * LANES, columns), np.float32)
    c = np.arange(columns)
    r, lane = c % CELL, c // CELL + LEAD
    out[(r % 4) * LANES + np.where(r < 4, lane, (lane + COLS) % LANES), c] = 1.0
    return jnp.asarray(out, jnp.bfloat16)


VMEM = pl.BlockSpec(memory_space=pltpu.VMEM)
ANY = pl.BlockSpec(memory_space=pl.ANY)


def shaped(*dims):
    return jax.ShapeDtypeStruct(dims, jnp.float32)


def planes(n, more=0, rows=ROWS):
    return (n + more, n, rows, LANES)


def buffers(*shapes):
    return [pltpu.VMEM(s, jnp.float32) for s in shapes]


def limit(mib):
    return pltpu.CompilerParams(vmem_limit_bytes=mib * 1024 * 1024)


def cost(flops, moved):
    return pl.CostEstimate(flops=flops, bytes_accessed=moved, transcendentals=0)


def local(right_side, depth_level, ocean_mask):
    rows, columns = right_side.shape
    lon, lat = lax.axis_size("lon"), lax.axis_size("lat")
    side = pltpu.VMEM((2, rows, LANES), jnp.float32), pltpu.VMEM((2, rows, LANES), jnp.int32)
    first, second = pl.pallas_call(
        pack_kernel,
        out_shape=[shaped(2, 3 * rows // 4, LANES)] * 2,
        in_specs=[ANY] * 3,
        out_specs=[VMEM] * 2,
        scratch_shapes=[side[0], side[1], side[1], pltpu.SemaphoreType.DMA((2, 3))],
        compiler_params=limit(58),
    )(right_side, depth_level, ocean_mask)
    first = swap(first, "lon", lon, 0, True)
    second = swap(second, "lon", lon, 1, True)
    tiles = (columns // LANES, rows, LANES)
    own = pl.pallas_call(
        own_kernel,
        out_shape=[shaped(*planes(8))] * 2,
        in_specs=[VMEM] * 4,
        out_specs=[VMEM] * 2,
        scratch_shapes=buffers(tiles, tiles),
        compiler_params=limit(16),
        cost_estimate=cost(8 * rows * columns * CELL * LANES, 16 * rows * columns),
    )(right_side, depth_level, ocean_mask, own_matrix(columns))

    message = shaped(6 * CELL + 4, 8, LANES)
    levels = (8, 4, 2)
    coefficients = [s for n in levels for s in (planes(n), planes(n, 1), planes(n), planes(n), planes(n))]
    fields = [s for n in levels for s in (planes(n), planes(n, 1))] + [(2, ROWS, LANES)] + [planes(n, 2) for n in levels]
    *fields, first, second = pl.pallas_call(
        down_kernel,
        out_shape=[shaped(*s) for s in fields + coefficients] + [message] * 2,
        in_specs=[VMEM] * 5,
        out_specs=[VMEM] * (len(fields) + len(coefficients) + 2),
        scratch_shapes=buffers(*[planes(n, 2) for n in levels]),
        compiler_params=limit(24),
    )(first, second, *own, side_matrix(columns))
    first = swap(first, "lat", lat, 0, False)
    second = swap(second, "lat", lat, 1, False)
    return pl.pallas_call(
        up_kernel,
        out_shape=[shaped(rows, columns)] * 2,
        in_specs=[VMEM] * (len(fields) + 3),
        out_specs=[ANY] * 2,
        scratch_shapes=buffers(
            (2, 4, 8, LANES),
            *[
                s
                for n in levels
                for s in (
                    planes(n, 0, 24), planes(n, 1, 24), planes(n, 0, 24), planes(n, 1, 24),
                    planes(n, 0, 24), planes(n, 0, 24), planes(n, 0, 24),
                    planes(n, 2, 24), planes(n, 2, 24), planes(n, 2, TALL), planes(n, 2, TALL),
                )
            ],
            (rows, 4 * LANES), (2, *tiles),
        ) + [pltpu.SemaphoreType.DMA((2, columns // LANES))],
        compiler_params=limit(24),
    )(*fields, first, second, join_matrix(columns))


def solution(mesh):
    placed = (P("lat", "lon"), P("lat", "lon"), P("lat", "lon"))
    return jax.shard_map(
        local,
        mesh=mesh,
        in_specs=placed,
        out_specs=(P("lat", "lon"), P("lat", "lon")),
        check_vma=False,
    )
```

profile of v0, /device:TPU:1, one launch (start us, length us, event | category | flops | bytes accessed | tf_op | source)
XLA Modules:
  0.0 34.7 jit_solution(13277726426488844060)
XLA Ops:
  0.6 0.0 copy-start.2
  0.6 0.0 copy-start.1
  0.6 0.0 copy-start
  0.7 2.3 %shard_map.77 = (f32[2,192,128]{2,1,0:T(8,128)}, f32[2,192,128]{2,1,0:T(8,128)}) custom-call(f32[256,512]{1,0:T(8,128)} %f.3, s32[256,512]{1,0:T(8,128)} %depth.3, s32[256,512]{1,0:T(8,128)} %mask.3), custom_call_target="tpu_custom_call" | custom-call | tf_op jit(solution)/shard_map/pallas_call | solution.py:479
  3.0 2.2 %collective-permute-start = (f32[2,192,128]{2,1,0:T(8,128)}, f32[2,192,128]{2,1,0:T(8,128)S(1)}, u32[]{:S(2)}, u32[]{:S(2)}) collective-permute-start(f32[2,192,128]{2,1,0:T(8,128)} %get-tuple-element.33), channel_id=1, source_target_pairs={{0,8},{8,0},{16,24},{24,16},{32,40},{40,32},{48,56},{56,48},{64,72... | collective-permute-start | bytes 589832 | tf_op jit(solution)/shard_map/ppermute | solution.py:424
  5.2 0.0 copy-start.4
  5.2 7.2 %collective-permute-start.1 = (f32[2,192,128]{2,1,0:T(8,128)}, f32[2,192,128]{2,1,0:T(8,128)S(1)}, u32[]{:S(2)}, u32[]{:S(2)}) collective-permute-start(f32[2,192,128]{2,1,0:T(8,128)} %get-tuple-element.34), channel_id=1, source_target_pairs={{8,16},{16,8},{24,32},{32,24},{40,48},{48,40},{56,64},{64,56},{72,... | collective-permute-start | bytes 589832 | tf_op jit(solution)/shard_map/ppermute | solution.py:424
  12.4 0.0 copy-done.2
  12.4 0.0 copy-done.1
  12.4 0.0 copy-done
  12.4 0.0 copy-start.5
  12.4 1.2 %copy-done.5 = bf16[512,1024]{1,0:T(8,128)(2,1)S(1)} copy-done((bf16[512,1024]{1,0:T(8,128)(2,1)S(1)}, bf16[512,1024]{1,0:T(8,128)(2,1)}, u32[]{:S(2)}) %copy-start.5) | copy-done | bytes 1048600
  13.6 1.4 %shard_map.78 = (f32[8,8,32,128]{3,2,1,0:T(8,128)S(1)}, f32[8,8,32,128]{3,2,1,0:T(8,128)S(1)}) custom-call(f32[256,512]{1,0:T(8,128)S(1)} %copy-done, s32[256,512]{1,0:T(8,128)S(1)} %copy-done.1, s32[256,512]{1,0:T(8,128)S(1)} %copy-done.2, bf16[512,1024]{1,0:T(8,128)(2,1)S(1)} %copy-done.5), custom_call_target="tpu_custom_call" | custom-call | flops 1073741824 | bytes 2097152 | tf_op jit(solution)/shard_map/pallas_call | solution.py:490
  15.0 0.0 collective-permute-done.first
  15.0 1.9 %collective-permute-done.1.second = f32[2,192,128]{2,1,0:T(8,128)S(1)} collective-permute-done((f32[2,192,128]{2,1,0:T(8,128)}, f32[2,192,128]{2,1,0:T(8,128)S(1)}, u32[]{:S(2)}, u32[]{:S(2)}) %collective-permute-start.1) | collective-permute-done | bytes 196640 | tf_op jit(solution)/shard_map/ppermute | solution.py:424
  16.9 0.0 copy-done.4
  16.9 0.0 copy-start.3
  16.9 3.2 %shard_map.79 = (f32[8,8,32,128]{3,2,1,0:T(8,128)S(1)}, f32[9,8,32,128]{3,2,1,0:T(8,128)S(1)}, f32[4,4,32,128]{3,2,1,0:T(8,128)S(1)}, f32[5,4,32,128]{3,2,1,0:T(...) custom-call(f32[2,192,128]{2,1,0:T(8,128)S(1)} %collective-permute-d, ...), custom_call_target="tpu_custom_call" | custom-call | tf_op jit(solution)/shard_map/pallas_call | solution.py:504
  20.1 1.6 %collective-permute-start.2 = (f32[52,8,128]{2,1,0:T(8,128)S(1)}, f32[52,8,128]{2,1,0:T(8,128)S(1)}, u32[]{:S(2)}, u32[]{:S(2)}) collective-permute-start(f32[52,8,128]{2,1,0:T(8,128)S(1)} %get-tuple-element.62), channel_id=1, source_target_pairs={{0,1},{1,0},{2,3},{3,2},{4,5},{5,4},{6,7},{7,6},{8,9},{9,8},{10,11... | collective-permute-start | bytes 638984 | tf_op jit(solution)/shard_map/ppermute | solution.py:424
  21.7 3.0 %collective-permute-start.3 = (f32[52,8,128]{2,1,0:T(8,128)S(1)}, f32[52,8,128]{2,1,0:T(8,128)S(1)}, u32[]{:S(2)}, u32[]{:S(2)}) collective-permute-start(f32[52,8,128]{2,1,0:T(8,128)S(1)} %get-tuple-element.63), channel_id=1, source_target_pairs={{1,2},{2,1},{3,4},{4,3},{5,6},{6,5},{9,10},{10,9},{11,12},{12,11},... | collective-permute-start | bytes 638984 | tf_op jit(solution)/shard_map/ppermute | solution.py:424
  24.7 0.0 collective-permute-done.2.first
  24.7 4.1 %collective-permute-done.3.second = f32[52,8,128]{2,1,0:T(8,128)S(1)} collective-permute-done((f32[52,8,128]{2,1,0:T(8,128)S(1)}, f32[52,8,128]{2,1,0:T(8,128)S(1)}, u32[]{:S(2)}, u32[]{:S(2)}) %collective-permute-start.3) | collective-permute-done | bytes 213024 | tf_op jit(solution)/shard_map/ppermute | solution.py:424
  28.9 0.0 copy-done.3
  28.9 5.9 %shard_map.80 = (f32[256,512]{1,0:T(8,128)}, f32[256,512]{1,0:T(8,128)}) custom-call(f32[8,8,32,128]{3,2,1,0:T(8,128)S(1)} %get-tuple-element.37.s0_in, f32[9,8,32,128]{3,2,1,0:T(8,128)S(1)} %get-tuple-element.38.h0_in, f32[4,4,32,128]{3,2,1,0:T(8,128)S(1)} %get-tuple-element.39.s1_in, f32[5,4,32,128]{3,2,1,0:T(8,128)S(1)} %get-tuple-element.40.h1_in, ...), custom_call_target="tpu_custom_call" | custom-call | tf_op jit(solution)/shard_map/pallas_call | solution.py:514
Async XLA Ops:
  0.6 11.7 %copy-start.2 = (s32[256,512]{1,0:T(8,128)S(1)}, s32[256,512]{1,0:T(8,128)}, u32[]{:S(2)}) copy-start(s32[256,512]{1,0:T(8,128)} %mask.3) | copy-start | bytes 1572868
  0.6 11.7 %copy-start.1 = (s32[256,512]{1,0:T(8,128)S(1)}, s32[256,512]{1,0:T(8,128)}, u32[]{:S(2)}) copy-start(s32[256,512]{1,0:T(8,128)} %depth.3) | copy-start | bytes 1572868
  0.6 11.7 %copy-start = (f32[256,512]{1,0:T(8,128)S(1)}, f32[256,512]{1,0:T(8,128)}, u32[]{:S(2)}) copy-start(f32[256,512]{1,0:T(8,128)} %f.3) | copy-start | bytes 1572868
  3.0 12.0 %collective-permute-start = (f32[2,192,128]{2,1,0:T(8,128)}, f32[2,192,128]{2,1,0:T(8,128)S(1)}, u32[]{:S(2)}, u32[]{:S(2)}) collective-permute-start(f32[2,192,128]{2,1,0:T(8,128)} %get-tuple-element.33), channel_id=1, source_target_pairs={{0,8},{8,0},{16,24},{24,16},{32,40},{40,32},{48,56},{56,48},{64,72... | collective-permute-start | bytes 589832 | tf_op jit(solution)/shard_map/ppermute | solution.py:424
  5.2 11.7 %copy-start.4 = (bf16[256,1024]{1,0:T(8,128)(2,1)S(1)}, bf16[256,1024]{1,0:T(8,128)(2,1)}, u32[]{:S(2)}) copy-start(bf16[256,1024]{1,0:T(8,128)(2,1)} %constant.7.clone.split) | copy-start | bytes 1572868
  5.2 11.7 %collective-permute-start.1 = (f32[2,192,128]{2,1,0:T(8,128)}, f32[2,192,128]{2,1,0:T(8,128)S(1)}, u32[]{:S(2)}, u32[]{:S(2)}) collective-permute-start(f32[2,192,128]{2,1,0:T(8,128)} %get-tuple-element.34), channel_id=1, source_target_pairs={{8,16},{16,8},{24,32},{32,24},{40,48},{48,40},{56,64},{64,56},{72,... | collective-permute-start | bytes 589832 | tf_op jit(solution)/shard_map/ppermute | solution.py:424
  12.4 1.2 %copy-start.5 = (bf16[512,1024]{1,0:T(8,128)(2,1)S(1)}, bf16[512,1024]{1,0:T(8,128)(2,1)}, u32[]{:S(2)}) copy-start(bf16[512,1024]{1,0:T(8,128)(2,1)} %constant.6.clone.split) | copy-start | bytes 3145732
  16.9 12.0 %copy-start.3 = (bf16[512,512]{1,0:T(8,128)(2,1)S(1)}, bf16[512,512]{1,0:T(8,128)(2,1)}, u32[]{:S(2)}) copy-start(bf16[512,512]{1,0:T(8,128)(2,1)} %constant.8.clone.join) | copy-start | bytes 1572868
  20.1 4.7 %collective-permute-start.2 = (f32[52,8,128]{2,1,0:T(8,128)S(1)}, f32[52,8,128]{2,1,0:T(8,128)S(1)}, u32[]{:S(2)}, u32[]{:S(2)}) collective-permute-start(f32[52,8,128]{2,1,0:T(8,128)S(1)} %get-tuple-element.62), channel_id=1, source_target_pairs={{0,1},{1,0},{2,3},{3,2},{4,5},{5,4},{6,7},{7,6},{8,9},{9,8},{10,11... | collective-permute-start | bytes 638984 | tf_op jit(solution)/shard_map/ppermute | solution.py:424
  21.7 7.2 %collective-permute-start.3 = (f32[52,8,128]{2,1,0:T(8,128)S(1)}, f32[52,8,128]{2,1,0:T(8,128)S(1)}, u32[]{:S(2)}, u32[]{:S(2)}) collective-permute-start(f32[52,8,128]{2,1,0:T(8,128)S(1)} %get-tuple-element.63), channel_id=1, source_target_pairs={{1,2},{2,1},{3,4},{4,3},{5,6},{6,5},{9,10},{10,9},{11,12},{12,11},... | collective-permute-start | bytes 638984 | tf_op jit(solution)/shard_map/ppermute | solution.py:424
where the time goes:
time: 34.9 us; the launch traced here: 34.7 us
  starting transfers between devices  14.1 us (40%)
  Pallas kernels  12.7 us (36%)
  waiting for transfers between devices  5.99 us (17%)
  local copies, waits for them, and re-layouts  1.24 us (4%)
  between operations  0.71 us (2%)
    ppermute x4, starting transfers between devices, swap(): return lax.ppermute(x, axis, pairs)  14.1 us
    ppermute x4, waiting for transfers between devices, swap(): return lax.ppermute(x, axis, pairs)  5.99 us
    pallas_call x1, Pallas kernels, local(): pl.pallas_call(up_kernel, out_shape=[shaped(rows, columns)] * 2, in_specs...  5.86 us
    pallas_call x1, Pallas kernels, local(): pl.pallas_call(down_kernel, out_shape=[shaped(*s) for s in fields + coeff...  3.18 us
    pallas_call x1, Pallas kernels, local(): pl.pallas_call(pack_kernel, out_shape=[shaped(2, 3 * rows // 4, LANES)] *...  2.29 us
    pallas_call x1, Pallas kernels, local(): pl.pallas_call(own_kernel, out_shape=[shaped(*planes(8))] * 2, in_specs=[...  1.39 us
    unnamed x12, local copies, waits for them, and re-layouts  1.24 us
  transfers between devices with their start and end apart: 4, of which 2 were waited for; matrix products, arithmetic and copies ran while one was open for 0% of the time, Pallas kernels for 4%

commit v1 on v0

--- a/solution.py
+++ b/solution.py
@@ -203,8 +203,11 @@
     by_parity("lon", fill, first, second)
 
 
-def own_kernel(f, depth, mask, split, s0, h0, nat_s, nat_h):
-    matrix = split[...]
+def own_kernel(f, depth, mask, s0, h0, nat_s, nat_h):
+    lane = lax.broadcasted_iota(jnp.int32, (1, CELL * LANES), 1)
+    column = CELL * ((lane & (LANES - 1)) - LEAD) + lane // LANES
+    row = lax.broadcasted_iota(jnp.int32, (f.shape[1], CELL * LANES), 0)
+    matrix = jnp.where(row == column, 1.0, 0.0).astype(jnp.bfloat16)
     tiles = nat_s.shape[0]
     for c in range(tiles):
         lanes = slice(c * LANES, (c + 1) * LANES)
@@ -223,7 +226,7 @@
 def down_kernel(
     first, second, s_own, h_own, split,
     s0, h0, s1, h1, s2, h2, s3, it0, it1, it2,
-    ke0, kn0, d0, w0, k0, ke1, kn1, d1, w1, k1, ke2, kn2, d2, w2, k2, out_first, out_second,
+    ke0, kn0, d0, w0, k0, ke1, kn1, d1, w1, k1, ke2, kn2, d2, w2, k2, out_second, out_first,
     v0, v1, v2,
 ):
     even = lax.rem(lax.axis_index("lon"), 2) == 0
@@ -296,7 +299,7 @@
 def up_kernel(
     s0_in, h0_in, s1_in, h1_in, s2_in, h2_in, s3_in, it0_in, it1_in, it2_in,
     ke0_in, kn0_in, d0_in, w0_in, k0_in, ke1_in, kn1_in, d1_in, w1_in, k1_in, ke2_in, kn2_in, d2_in, w2_in, k2_in,
-    first, second, join,
+    second, first, join,
     pressure, residual,
     far, s0, h0, ke0, kn0, d0, w0, k0, e0, g0, a0, b0,
     s1, h1, ke1, kn1, d1, w1, k1, e1, g1, a1, b1, s2, h2, ke2, kn2, d2, w2, k2, e2, g2, a2, b2, flat, nat, sems,
@@ -424,13 +427,6 @@
     return lax.ppermute(x, axis, pairs)
 
 
-def own_matrix(columns):
-    out = np.zeros((columns, CELL * LANES), np.float32)
-    c = np.arange(columns)
-    out[c, (c % CELL) * LANES + LEAD + c // CELL] = 1.0
-    return jnp.asarray(out, jnp.bfloat16)
-
-
 def side_matrix(columns):
     out = np.zeros((2 * LANES, CELL * LANES), np.float32)
     c = np.arange(LANES - SIDE, LANES)
@@ -490,18 +486,18 @@
     own = pl.pallas_call(
         own_kernel,
         out_shape=[shaped(*planes(8))] * 2,
-        in_specs=[VMEM] * 4,
+        in_specs=[VMEM] * 3,
         out_specs=[VMEM] * 2,
         scratch_shapes=buffers(tiles, tiles),
         compiler_params=limit(16),
         cost_estimate=cost(8 * rows * columns * CELL * LANES, 16 * rows * columns),
-    )(right_side, depth_level, ocean_mask, own_matrix(columns))
+    )(right_side, depth_level, ocean_mask)
 
     message = shaped(6 * CELL + 4, 8, LANES)
     levels = (8, 4, 2)
     coefficients = [s for n in levels for s in (planes(n), planes(n, 1), planes(n), planes(n), planes(n))]
     fields = [s for n in levels for s in (planes(n), planes(n, 1))] + [(2, ROWS, LANES)] + [planes(n, 2) for n in levels]
-    *fields, first, second = pl.pallas_call(
+    *fields, second, first = pl.pallas_call(
         down_kernel,
         out_shape=[shaped(*s) for s in fields + coefficients] + [message] * 2,
         in_specs=[VMEM] * 5,
@@ -509,8 +505,8 @@
         scratch_shapes=buffers(*[planes(n, 2) for n in levels]),
         compiler_params=limit(24),
     )(first, second, *own, side_matrix(columns))
+    second = swap(second, "lat", lat, 1, False)
     first = swap(first, "lat", lat, 0, False)
-    second = swap(second, "lat", lat, 1, False)
     return pl.pallas_call(
         up_kernel,
         out_shape=[shaped(rows, columns)] * 2,
@@ -530,7 +526,7 @@
             (rows, 4 * LANES), (2, *tiles),
         ) + [pltpu.SemaphoreType.DMA((2, columns // LANES))],
         compiler_params=limit(24),
-    )(*fields, first, second, join_matrix(columns))
+    )(*fields, second, first, join_matrix(columns))
 
 
 def solution(mesh):

time: 34.9 us -> 34.1 us (0.977)
  local copies, waits for them, and re-layouts: 1.24 us -> 0.02 us
  waiting for transfers between devices: 5.99 us -> 6.49 us
    unnamed x12 -> x10, local copies, waits for them, and re-layouts: 1.24 us -> 0.02 us
    ppermute x4, waiting for transfers between devices: 5.99 us -> 6.49 us  [swap(): return lax.ppermute(x, axis, pairs)]
where the time goes in v1:
time: 34.1 us; the launch traced here: 34 us
  starting transfers between devices  14.1 us (41%)
  Pallas kernels  12.7 us (37%)
  waiting for transfers between devices  6.49 us (19%)
  between operations  0.7 us (2%)
    ppermute x4, starting transfers between devices, swap(): return lax.ppermute(x, axis, pairs)  14.1 us
    ppermute x4, waiting for transfers between devices, swap(): return lax.ppermute(x, axis, pairs)  6.49 us
    pallas_call x1, Pallas kernels, local(): pl.pallas_call(up_kernel, out_shape=[shaped(rows, columns)] * 2, in_specs...  5.87 us
    pallas_call x1, Pallas kernels, local(): pl.pallas_call(down_kernel, out_shape=[shaped(*s) for s in fields + coeff...  3.18 us
    pallas_call x1, Pallas kernels, local(): pl.pallas_call(pack_kernel, out_shape=[shaped(2, 3 * rows // 4, LANES)] *...  2.29 us
    pallas_call x1, Pallas kernels, local(): pl.pallas_call(own_kernel, out_shape=[shaped(*planes(8))] * 2, in_specs=[...  1.42 us
  transfers between devices with their start and end apart: 4, of which 2 were waited for; matrix products, arithmetic and copies ran while one was open for 0% of the time, Pallas kernels for 4%

profile of v1, /device:TPU:1, one launch (start us, length us, event | category | flops | bytes accessed | tf_op | source)
XLA Modules:
  0.0 34.0 jit_solution(12954198889816861227)
XLA Ops:
  0.6 0.0 copy-start.2
  0.6 0.0 copy-start.1
  0.6 0.0 copy-start
  0.7 2.3 %shard_map.68 = (f32[2,192,128]{2,1,0:T(8,128)}, f32[2,192,128]{2,1,0:T(8,128)}) custom-call(f32[256,512]{1,0:T(8,128)} %f.3, s32[256,512]{1,0:T(8,128)} %depth.3, s32[256,512]{1,0:T(8,128)} %mask.3), custom_call_target="tpu_custom_call" | custom-call | tf_op jit(solution)/shard_map/pallas_call | solution.py:475
  3.0 2.2 %collective-permute-start = (f32[2,192,128]{2,1,0:T(8,128)}, f32[2,192,128]{2,1,0:T(8,128)S(1)}, u32[]{:S(2)}, u32[]{:S(2)}) collective-permute-start(f32[2,192,128]{2,1,0:T(8,128)} %get-tuple-element.33), channel_id=1, source_target_pairs={{0,8},{8,0},{16,24},{24,16},{32,40},{40,32},{48,56},{56,48},{64,72... | collective-permute-start | bytes 589832 | tf_op jit(solution)/shard_map/ppermute | solution.py:427
  5.2 0.0 copy-start.4
  5.2 7.2 %collective-permute-start.1 = (f32[2,192,128]{2,1,0:T(8,128)}, f32[2,192,128]{2,1,0:T(8,128)S(1)}, u32[]{:S(2)}, u32[]{:S(2)}) collective-permute-start(f32[2,192,128]{2,1,0:T(8,128)} %get-tuple-element.34), channel_id=1, source_target_pairs={{8,16},{16,8},{24,32},{32,24},{40,48},{48,40},{56,64},{64,56},{72,... | collective-permute-start | bytes 589832 | tf_op jit(solution)/shard_map/ppermute | solution.py:427
  12.4 0.0 copy-done.2
  12.4 0.0 copy-done.1
  12.4 0.0 copy-done
  12.4 1.4 %shard_map.69 = (f32[8,8,32,128]{3,2,1,0:T(8,128)S(1)}, f32[8,8,32,128]{3,2,1,0:T(8,128)S(1)}) custom-call(f32[256,512]{1,0:T(8,128)S(1)} %copy-done, s32[256,512]{1,0:T(8,128)S(1)} %copy-done.1, s32[256,512]{1,0:T(8,128)S(1)} %copy-done.2), custom_call_target="tpu_custom_call" | custom-call | flops 1073741824 | bytes 2097152 | tf_op jit(solution)/shard_map/pallas_call | solution.py:486
  13.8 0.0 collective-permute-done.first
  13.8 3.1 %collective-permute-done.1.second = f32[2,192,128]{2,1,0:T(8,128)S(1)} collective-permute-done((f32[2,192,128]{2,1,0:T(8,128)}, f32[2,192,128]{2,1,0:T(8,128)S(1)}, u32[]{:S(2)}, u32[]{:S(2)}) %collective-permute-start.1) | collective-permute-done | bytes 196640 | tf_op jit(solution)/shard_map/ppermute | solution.py:427
  16.9 0.0 copy-done.4
  16.9 0.0 copy-start.3
  16.9 3.2 %shard_map.70 = (f32[8,8,32,128]{3,2,1,0:T(8,128)S(1)}, f32[9,8,32,128]{3,2,1,0:T(8,128)S(1)}, f32[4,4,32,128]{3,2,1,0:T(8,128)S(1)}, f32[5,4,32,128]{3,2,1,0:T(...) custom-call(f32[2,192,128]{2,1,0:T(8,128)S(1)} %collective-permute-d, ...), custom_call_target="tpu_custom_call" | custom-call | tf_op jit(solution)/shard_map/pallas_call | solution.py:500
  20.1 4.6 %collective-permute-start.2 = (f32[52,8,128]{2,1,0:T(8,128)S(1)}, f32[52,8,128]{2,1,0:T(8,128)S(1)}, u32[]{:S(2)}, u32[]{:S(2)}) collective-permute-start(f32[52,8,128]{2,1,0:T(8,128)S(1)} %get-tuple-element.62), channel_id=1, source_target_pairs={{1,2},{2,1},{3,4},{4,3},{5,6},{6,5},{9,10},{10,9},{11,12},{12,11},... | collective-permute-start | bytes 638984 | tf_op jit(solution)/shard_map/ppermute | solution.py:427
  24.6 0.1 collective-permute-start.3
  24.7 3.4 %collective-permute-done.2.second = f32[52,8,128]{2,1,0:T(8,128)S(1)} collective-permute-done((f32[52,8,128]{2,1,0:T(8,128)S(1)}, f32[52,8,128]{2,1,0:T(8,128)S(1)}, u32[]{:S(2)}, u32[]{:S(2)}) %collective-permute-start.2) | collective-permute-done | bytes 213024 | tf_op jit(solution)/shard_map/ppermute | solution.py:427
  28.1 0.0 collective-permute-done.3.first
  28.2 0.0 copy-done.3
  28.2 5.9 %shard_map.71 = (f32[256,512]{1,0:T(8,128)}, f32[256,512]{1,0:T(8,128)}) custom-call(f32[8,8,32,128]{3,2,1,0:T(8,128)S(1)} %get-tuple-element.37.s0_in, f32[9,8,32,128]{3,2,1,0:T(8,128)S(1)} %get-tuple-element.38.h0_in, f32[4,4,32,128]{3,2,1,0:T(8,128)S(1)} %get-tuple-element.39.s1_in, f32[5,4,32,128]{3,2,1,0:T(8,128)S(1)} %get-tuple-element.40.h1_in, ...), custom_call_target="tpu_custom_call" | custom-call | tf_op jit(solution)/shard_map/pallas_call | solution.py:510
Async XLA Ops:
  0.6 11.7 %copy-start.2 = (s32[256,512]{1,0:T(8,128)S(1)}, s32[256,512]{1,0:T(8,128)}, u32[]{:S(2)}) copy-start(s32[256,512]{1,0:T(8,128)} %mask.3) | copy-start | bytes 1572868
  0.6 11.7 %copy-start.1 = (s32[256,512]{1,0:T(8,128)S(1)}, s32[256,512]{1,0:T(8,128)}, u32[]{:S(2)}) copy-start(s32[256,512]{1,0:T(8,128)} %depth.3) | copy-start | bytes 1572868
  0.6 11.7 %copy-start = (f32[256,512]{1,0:T(8,128)S(1)}, f32[256,512]{1,0:T(8,128)}, u32[]{:S(2)}) copy-start(f32[256,512]{1,0:T(8,128)} %f.3) | copy-start | bytes 1572868
  3.0 10.8 %collective-permute-start = (f32[2,192,128]{2,1,0:T(8,128)}, f32[2,192,128]{2,1,0:T(8,128)S(1)}, u32[]{:S(2)}, u32[]{:S(2)}) collective-permute-start(f32[2,192,128]{2,1,0:T(8,128)} %get-tuple-element.33), channel_id=1, source_target_pairs={{0,8},{8,0},{16,24},{24,16},{32,40},{40,32},{48,56},{56,48},{64,72... | collective-permute-start | bytes 589832 | tf_op jit(solution)/shard_map/ppermute | solution.py:427
  5.2 11.7 %copy-start.4 = (bf16[256,1024]{1,0:T(8,128)(2,1)S(1)}, bf16[256,1024]{1,0:T(8,128)(2,1)}, u32[]{:S(2)}) copy-start(bf16[256,1024]{1,0:T(8,128)(2,1)} %constant.4.clone.split) | copy-start | bytes 1572868
  5.2 11.7 %collective-permute-start.1 = (f32[2,192,128]{2,1,0:T(8,128)}, f32[2,192,128]{2,1,0:T(8,128)S(1)}, u32[]{:S(2)}, u32[]{:S(2)}) collective-permute-start(f32[2,192,128]{2,1,0:T(8,128)} %get-tuple-element.34), channel_id=1, source_target_pairs={{8,16},{16,8},{24,32},{32,24},{40,48},{48,40},{56,64},{64,56},{72,... | collective-permute-start | bytes 589832 | tf_op jit(solution)/shard_map/ppermute | solution.py:427
  16.9 11.3 %copy-start.3 = (bf16[512,512]{1,0:T(8,128)(2,1)S(1)}, bf16[512,512]{1,0:T(8,128)(2,1)}, u32[]{:S(2)}) copy-start(bf16[512,512]{1,0:T(8,128)(2,1)} %constant.5.clone.join) | copy-start | bytes 1572868
  20.1 8.1 %collective-permute-start.2 = (f32[52,8,128]{2,1,0:T(8,128)S(1)}, f32[52,8,128]{2,1,0:T(8,128)S(1)}, u32[]{:S(2)}, u32[]{:S(2)}) collective-permute-start(f32[52,8,128]{2,1,0:T(8,128)S(1)} %get-tuple-element.62), channel_id=1, source_target_pairs={{1,2},{2,1},{3,4},{4,3},{5,6},{6,5},{9,10},{10,9},{11,12},{12,11},... | collective-permute-start | bytes 638984 | tf_op jit(solution)/shard_map/ppermute | solution.py:427
  24.6 3.5 %collective-permute-start.3 = (f32[52,8,128]{2,1,0:T(8,128)S(1)}, f32[52,8,128]{2,1,0:T(8,128)S(1)}, u32[]{:S(2)}, u32[]{:S(2)}) collective-permute-start(f32[52,8,128]{2,1,0:T(8,128)S(1)} %get-tuple-element.63), channel_id=1, source_target_pairs={{0,1},{1,0},{2,3},{3,2},{4,5},{5,4},{6,7},{7,6},{8,9},{9,8},{10,11... | collective-permute-start | bytes 638984 | tf_op jit(solution)/shard_map/ppermute | solution.py:427

commit v2 on v1

--- a/solution.py
+++ b/solution.py
@@ -81,7 +81,7 @@
 
 def weigh(faces, source):
     diagonal = SIGMA + faces
-    return diagonal, OMEGA / diagonal, jnp.where(faces > 0.0, source, 0.0)
+    return diagonal, OMEGA * pl.reciprocal(diagonal), jnp.where(faces > 0.0, source, 0.0)
 
 
 def find_weights(n, ke, kn, source, d, w, s, v):
@@ -107,7 +107,7 @@
     return cs, out
 
 
-def sweep(n, ke, kn, w, s, v, out, also=None):
+def sweep(n, ke, kn, w, s, v, out, also=None, final=False):
     for q in range(n):
         cs, total = pull(n, ke, kn, v, q)
         for r in range(n):
@@ -115,7 +115,8 @@
             out[q + 1, r] = new
         if also is not None:
             also(q, [out[q + 1, r][:ROWS] for r in range(n)])
-    close(out, n)
+    if not final:
+        close(out, n)
 
 
 def remains(n, ke, kn, d, s, v, q, count=None):
@@ -381,7 +382,7 @@
         ke, kn, w, k = (Whole(x, y) for x, y in zip((inner[0], inner[1], inner[3], inner[4]), (ke, kn, w, k)))
         sweep(n, ke, kn, w, k, a, b)
         if n < CELL:
-            sweep(n, ke, kn, w, k, b, a)
+            sweep(n, ke, kn, w, k, b, a, final=True)
         above = lambda q, r, a=a: a[q + 1, r]
 
     def flatten(q, xs):

time: 34.1 us -> 34.1 us (level)
  no operation moved by 1% of the time
where the time goes in v2:
time: 34.1 us; the launch traced here: 34 us
  starting transfers between devices  14.1 us (41%)
  Pallas kernels  12.7 us (37%)
  waiting for transfers between devices  6.49 us (19%)
  between operations  0.7 us (2%)
    ppermute x4, starting transfers between devices, swap(): return lax.ppermute(x, axis, pairs)  14.1 us
    ppermute x4, waiting for transfers between devices, swap(): return lax.ppermute(x, axis, pairs)  6.49 us
    pallas_call x1, Pallas kernels, local(): pl.pallas_call(up_kernel, out_shape=[shaped(rows, columns)] * 2, in_specs...  5.87 us
    pallas_call x1, Pallas kernels, local(): pl.pallas_call(down_kernel, out_shape=[shaped(*s) for s in fields + coeff...  3.18 us
    pallas_call x1, Pallas kernels, local(): pl.pallas_call(pack_kernel, out_shape=[shaped(2, 3 * rows // 4, LANES)] *...  2.29 us
    pallas_call x1, Pallas kernels, local(): pl.pallas_call(own_kernel, out_shape=[shaped(*planes(8))] * 2, in_specs=[...  1.42 us
  transfers between devices with their start and end apart: 4, of which 2 were waited for; matrix products, arithmetic and copies ran while one was open for 0% of the time, Pallas kernels for 4%

profile of v2, /device:TPU:1, one launch (start us, length us, event | category | flops | bytes accessed | tf_op | source)
XLA Modules:
  0.0 34.0 jit_solution(12954198889816861227)
XLA Ops:
  0.6 0.0 copy-start.2
  0.6 0.0 copy-start.1
  0.6 0.0 copy-start
  0.7 2.3 %shard_map.68 = (f32[2,192,128]{2,1,0:T(8,128)}, f32[2,192,128]{2,1,0:T(8,128)}) custom-call(f32[256,512]{1,0:T(8,128)} %f.3, s32[256,512]{1,0:T(8,128)} %depth.3, s32[256,512]{1,0:T(8,128)} %mask.3), custom_call_target="tpu_custom_call" | custom-call | tf_op jit(solution)/shard_map/pallas_call | solution.py:476
  3.0 2.2 %collective-permute-start = (f32[2,192,128]{2,1,0:T(8,128)}, f32[2,192,128]{2,1,0:T(8,128)S(1)}, u32[]{:S(2)}, u32[]{:S(2)}) collective-permute-start(f32[2,192,128]{2,1,0:T(8,128)} %get-tuple-element.33), channel_id=1, source_target_pairs={{0,8},{8,0},{16,24},{24,16},{32,40},{40,32},{48,56},{56,48},{64,72... | collective-permute-start | bytes 589832 | tf_op jit(solution)/shard_map/ppermute | solution.py:428
  5.2 0.0 copy-start.4
  5.2 7.2 %collective-permute-start.1 = (f32[2,192,128]{2,1,0:T(8,128)}, f32[2,192,128]{2,1,0:T(8,128)S(1)}, u32[]{:S(2)}, u32[]{:S(2)}) collective-permute-start(f32[2,192,128]{2,1,0:T(8,128)} %get-tuple-element.34), channel_id=1, source_target_pairs={{8,16},{16,8},{24,32},{32,24},{40,48},{48,40},{56,64},{64,56},{72,... | collective-permute-start | bytes 589832 | tf_op jit(solution)/shard_map/ppermute | solution.py:428
  12.4 0.0 copy-done.2
  12.4 0.0 copy-done.1
  12.4 0.0 copy-done
  12.4 1.4 %shard_map.69 = (f32[8,8,32,128]{3,2,1,0:T(8,128)S(1)}, f32[8,8,32,128]{3,2,1,0:T(8,128)S(1)}) custom-call(f32[256,512]{1,0:T(8,128)S(1)} %copy-done, s32[256,512]{1,0:T(8,128)S(1)} %copy-done.1, s32[256,512]{1,0:T(8,128)S(1)} %copy-done.2), custom_call_target="tpu_custom_call" | custom-call | flops 1073741824 | bytes 2097152 | tf_op jit(solution)/shard_map/pallas_call | solution.py:487
  13.8 0.0 collective-permute-done.first
  13.8 3.1 %collective-permute-done.1.second = f32[2,192,128]{2,1,0:T(8,128)S(1)} collective-permute-done((f32[2,192,128]{2,1,0:T(8,128)}, f32[2,192,128]{2,1,0:T(8,128)S(1)}, u32[]{:S(2)}, u32[]{:S(2)}) %collective-permute-start.1) | collective-permute-done | bytes 196640 | tf_op jit(solution)/shard_map/ppermute | solution.py:428
  16.9 0.0 copy-done.4
  16.9 0.0 copy-start.3
  16.9 3.2 %shard_map.70 = (f32[8,8,32,128]{3,2,1,0:T(8,128)S(1)}, f32[9,8,32,128]{3,2,1,0:T(8,128)S(1)}, f32[4,4,32,128]{3,2,1,0:T(8,128)S(1)}, f32[5,4,32,128]{3,2,1,0:T(...) custom-call(f32[2,192,128]{2,1,0:T(8,128)S(1)} %collective-permute-d, ...), custom_call_target="tpu_custom_call" | custom-call | tf_op jit(solution)/shard_map/pallas_call | solution.py:501
  20.1 4.6 %collective-permute-start.2 = (f32[52,8,128]{2,1,0:T(8,128)S(1)}, f32[52,8,128]{2,1,0:T(8,128)S(1)}, u32[]{:S(2)}, u32[]{:S(2)}) collective-permute-start(f32[52,8,128]{2,1,0:T(8,128)S(1)} %get-tuple-element.62), channel_id=1, source_target_pairs={{1,2},{2,1},{3,4},{4,3},{5,6},{6,5},{9,10},{10,9},{11,12},{12,11},... | collective-permute-start | bytes 638984 | tf_op jit(solution)/shard_map/ppermute | solution.py:428
  24.6 0.1 collective-permute-start.3
  24.7 3.4 %collective-permute-done.2.second = f32[52,8,128]{2,1,0:T(8,128)S(1)} collective-permute-done((f32[52,8,128]{2,1,0:T(8,128)S(1)}, f32[52,8,128]{2,1,0:T(8,128)S(1)}, u32[]{:S(2)}, u32[]{:S(2)}) %collective-permute-start.2) | collective-permute-done | bytes 213024 | tf_op jit(solution)/shard_map/ppermute | solution.py:428
  28.1 0.0 collective-permute-done.3.first
  28.2 0.0 copy-done.3
  28.2 5.9 %shard_map.71 = (f32[256,512]{1,0:T(8,128)}, f32[256,512]{1,0:T(8,128)}) custom-call(f32[8,8,32,128]{3,2,1,0:T(8,128)S(1)} %get-tuple-element.37.s0_in, f32[9,8,32,128]{3,2,1,0:T(8,128)S(1)} %get-tuple-element.38.h0_in, f32[4,4,32,128]{3,2,1,0:T(8,128)S(1)} %get-tuple-element.39.s1_in, f32[5,4,32,128]{3,2,1,0:T(8,128)S(1)} %get-tuple-element.40.h1_in, ...), custom_call_target="tpu_custom_call" | custom-call | tf_op jit(solution)/shard_map/pallas_call | solution.py:511
Async XLA Ops:
  0.6 11.7 %copy-start.2 = (s32[256,512]{1,0:T(8,128)S(1)}, s32[256,512]{1,0:T(8,128)}, u32[]{:S(2)}) copy-start(s32[256,512]{1,0:T(8,128)} %mask.3) | copy-start | bytes 1572868
  0.6 11.7 %copy-start.1 = (s32[256,512]{1,0:T(8,128)S(1)}, s32[256,512]{1,0:T(8,128)}, u32[]{:S(2)}) copy-start(s32[256,512]{1,0:T(8,128)} %depth.3) | copy-start | bytes 1572868
  0.6 11.7 %copy-start = (f32[256,512]{1,0:T(8,128)S(1)}, f32[256,512]{1,0:T(8,128)}, u32[]{:S(2)}) copy-start(f32[256,512]{1,0:T(8,128)} %f.3) | copy-start | bytes 1572868
  3.0 10.8 %collective-permute-start = (f32[2,192,128]{2,1,0:T(8,128)}, f32[2,192,128]{2,1,0:T(8,128)S(1)}, u32[]{:S(2)}, u32[]{:S(2)}) collective-permute-start(f32[2,192,128]{2,1,0:T(8,128)} %get-tuple-element.33), channel_id=1, source_target_pairs={{0,8},{8,0},{16,24},{24,16},{32,40},{40,32},{48,56},{56,48},{64,72... | collective-permute-start | bytes 589832 | tf_op jit(solution)/shard_map/ppermute | solution.py:428
  5.2 11.7 %copy-start.4 = (bf16[256,1024]{1,0:T(8,128)(2,1)S(1)}, bf16[256,1024]{1,0:T(8,128)(2,1)}, u32[]{:S(2)}) copy-start(bf16[256,1024]{1,0:T(8,128)(2,1)} %constant.4.clone.split) | copy-start | bytes 1572868
  5.2 11.7 %collective-permute-start.1 = (f32[2,192,128]{2,1,0:T(8,128)}, f32[2,192,128]{2,1,0:T(8,128)S(1)}, u32[]{:S(2)}, u32[]{:S(2)}) collective-permute-start(f32[2,192,128]{2,1,0:T(8,128)} %get-tuple-element.34), channel_id=1, source_target_pairs={{8,16},{16,8},{24,32},{32,24},{40,48},{48,40},{56,64},{64,56},{72,... | collective-permute-start | bytes 589832 | tf_op jit(solution)/shard_map/ppermute | solution.py:428
  16.9 11.3 %copy-start.3 = (bf16[512,512]{1,0:T(8,128)(2,1)S(1)}, bf16[512,512]{1,0:T(8,128)(2,1)}, u32[]{:S(2)}) copy-start(bf16[512,512]{1,0:T(8,128)(2,1)} %constant.5.clone.join) | copy-start | bytes 1572868
  20.1 8.1 %collective-permute-start.2 = (f32[52,8,128]{2,1,0:T(8,128)S(1)}, f32[52,8,128]{2,1,0:T(8,128)S(1)}, u32[]{:S(2)}, u32[]{:S(2)}) collective-permute-start(f32[52,8,128]{2,1,0:T(8,128)S(1)} %get-tuple-element.62), channel_id=1, source_target_pairs={{1,2},{2,1},{3,4},{4,3},{5,6},{6,5},{9,10},{10,9},{11,12},{12,11},... | collective-permute-start | bytes 638984 | tf_op jit(solution)/shard_map/ppermute | solution.py:428
  24.6 3.5 %collective-permute-start.3 = (f32[52,8,128]{2,1,0:T(8,128)S(1)}, f32[52,8,128]{2,1,0:T(8,128)S(1)}, u32[]{:S(2)}, u32[]{:S(2)}) collective-permute-start(f32[52,8,128]{2,1,0:T(8,128)S(1)} %get-tuple-element.63), channel_id=1, source_target_pairs={{0,1},{1,0},{2,3},{3,2},{4,5},{5,4},{6,7},{7,6},{8,9},{9,8},{10,11... | collective-permute-start | bytes 638984 | tf_op jit(solution)/shard_map/ppermute | solution.py:428
